TPU v7x, 32 devices: a whole 2x2x4 slice. The times are simulated.
32 devices in a mesh: blk: 8 (over y, x, core), grp: 4 (over z).
Axes of the slice: x: 2, y: 2, z: 4, core: 2. Of those that a mesh axis runs over, the one named last changes fastest.
Arguments:
- states: float32 [54, 16384], P(None, ('blk', 'grp')), may hold values from 0 to 1
- lengthscales: float32 [54], replicated, may hold values from 0.4 to 1
- noise_var: float32 [1], replicated, may hold values from 0.5 to 1.5
- solution: float32 [32, 16384], P(None, ('blk', 'grp')), may hold values from -6 to 6
- residual: float32 [32, 16384], P(None, ('blk', 'grp')), may hold values from -6 to 6, as said below
- direction: float32 [32, 16384], P(None, ('blk', 'grp')), may hold values from -6 to 6, as said below
Outputs:
- new_solution: float32 [32, 16384], P(None, ('blk', 'grp'))
- new_residual: float32 [32, 16384], P(None, ('blk', 'grp'))
- new_direction: float32 [32, 16384], P(None, ('blk', 'grp'))
Inputs may be any that keep to these rules, and one draw needn't show every extreme that they name: `residual`: entries of order one. `direction`: entries of order one.
All inputs are finite; a program needn't handle non-finite values.
Results may differ from a plain program's by a relative error of at most 0.000071.
Values sent between devices are 32-bit elements; how exact they have to be, the bound alone decides.
A program may use at most 128 MiB of HBM per device.

v0:
```python
import math

import jax
import jax.numpy as jnp
from jax import lax
from jax.sharding import PartitionSpec as P


def matern_tile(rows_scaled, row_norm, cols_scaled):
    cross_term = jnp.dot(
        rows_scaled.T,
        cols_scaled,
        precision=lax.Precision.HIGHEST,
        preferred_element_type=jnp.float32,
    )
    column_norm_value = jnp.sum(cols_scaled * cols_scaled, axis=0)
    sqdist = jnp.maximum(row_norm[:, None] + column_norm_value[None, :] - 2.0 * cross_term, 0.0)
    spread = jnp.sqrt(5.0 * sqdist)
    return (1.0 + spread + spread * spread / 3.0) * jnp.exp(-spread)


def apply_kernel(batch_descent_vectors, kernel):
    return lax.dot_general(
        batch_descent_vectors,
        kernel,
        (((1,), (1,)), ((), ())),
        precision=lax.Precision.HIGHEST,
        preferred_element_type=jnp.float32,
    )


def apply_blocks(rows_scaled, row_norm, cols_scaled, batch_descent_vectors):
    columns = cols_scaled.shape[1]
    block_width = math.gcd(columns, 2048)
    block_count = columns // block_width

    def one_block(block_index, running):
        col_slab = lax.dynamic_slice_in_dim(cols_scaled, block_index * block_width, block_width, 1)
        dir_slab = lax.dynamic_slice_in_dim(
            batch_descent_vectors, block_index * block_width, block_width, 1
        )
        kernel = matern_tile(rows_scaled, row_norm, col_slab)
        return running + apply_kernel(dir_slab, kernel)

    empty = jnp.zeros((batch_descent_vectors.shape[0], rows_scaled.shape[1]), jnp.float32)
    return lax.fori_loop(0, block_count, one_block, empty)


def per_device(states, lengthscales, noise_var, solution, residual, direction):
    own_scaled = (states - 0.5) / lengthscales[:, None]
    own_norm = jnp.sum(own_scaled * own_scaled, axis=0)
    local_norm = jnp.sum(residual * residual, axis=1)
    old_norm = lax.psum(local_norm, ("blk", "grp"))
    col_scaled = (lax.all_gather(states, ("blk", "grp"), axis=1, tiled=True) - 0.5) / lengthscales[
        :, None
    ]
    image_sum = apply_blocks(
        own_scaled,
        own_norm,
        col_scaled,
        lax.all_gather(direction, ("blk", "grp"), axis=1, tiled=True),
    )
    image_sum = image_sum + noise_var[0] * direction
    local_curvature = jnp.sum(direction * image_sum, axis=1)
    curvature = lax.psum(local_curvature, ("blk", "grp"))
    step_size = old_norm / curvature
    new_solution = solution + step_size[:, None] * direction
    new_residual = residual - step_size[:, None] * image_sum
    new_norm = lax.psum(jnp.sum(new_residual * new_residual, axis=1), ("blk", "grp"))
    new_direction = new_residual + (new_norm / old_norm)[:, None] * direction
    return (new_solution, new_residual, new_direction)


def solution(mesh):
    in_specs = (
        P(None, ("blk", "grp")),
        P(),
        P(),
        P(None, ("blk", "grp")),
        P(None, ("blk", "grp")),
        P(None, ("blk", "grp")),
    )
    out_specs = (P(None, ("blk", "grp")), P(None, ("blk", "grp")), P(None, ("blk", "grp")))
    return jax.shard_map(
        per_device, mesh=mesh, in_specs=in_specs, out_specs=out_specs, check_vma=False
    )
```

profile of v0, /device:TPU:0, one launch (start us, length us, event | category | flops | bytes accessed | tf_op | source)
XLA Modules:
  0.0 329.4 jit_solution(4660677521639875570)
XLA Ops:
  7.2 0.0 all-gather.5.cloned.1.call-start
  7.2 0.7 all-gather.5.cloned.1.call-update
  7.9 0.0 all-gather.3.cloned.1.call-start
  7.9 0.7 all-gather.3.cloned.1.call-update
  9.3 1.0 multiply_reduce_fusion.1
  10.3 63.7 %all-gather.5.cloned.1.call-done = f32[54,16384]{1,0:T(8,128)} async-done(((f32[54,512]{1,0:T(8,128)}), f32[54,16384]{1,0:T(8,128)}) %all-gather.5.cloned.1.call-update) | async-done | bytes 3538960 | tf_op jit(solution)/shard_map/all_gather | solution.py:54
  74.0 4.2 %add_divide_fusion = f32[54,16384]{1,0:T(8,128)} fusion(f32[54,16384]{1,0:T(8,128)} %all-gather.5.cloned.1.call-done, f32[54]{0:T(128)} %param.9), kind=kLoop, calls=%fused_computation.33 | loop fusion | flops 1769472 | bytes 7078104 | tf_op jit(solution)/shard_map/div | solution.py:54
  78.2 53.8 %all-gather.3.cloned.1.call-done = f32[32,16384]{1,0:T(8,128)} async-done(((f32[32,512]{1,0:T(8,128)}), f32[32,16384]{1,0:T(8,128)}) %all-gather.3.cloned.1.call-update) | async-done | bytes 2097168 | tf_op jit(solution)/shard_map/all_gather | solution.py:61
  132.0 0.0 copy-start
  132.0 0.0 copy-start.1
  132.0 0.0 copy-start.3
  132.0 109.5 %while.14 = (s32[]{:T(128)}, f32[32,512]{1,0:T(8,128)S(1)}, f32[32,16384]{1,0:T(8,128)}, f32[512]{0:T(512)S(1)}, f32[54,16384]{1,0:T(8,128)}, /*index=5*/f32[54,...) while((s32[]{:T(128)}, f32[32,512]{1,0:T(8,128)S(1)}, f32[32,16384]{1,0:T(8,128)}, ...), condition=%wide.region_5.0_spmd.clone, body=%wide.region_3.0_spmd.clone.sunk | while | flops 1093916672 | bytes 9812137 | solution.py:46
  132.0 6.2 %fusion.45 = f32[2048,512]{1,0:T(8,128)} fusion(f32[54,512]{1,0:T(8,128)S(1)} %get-tuple-element.217, f32[54,16384]{1,0:T(8,128)} %get-tuple-element.216, s32[]{:T(128)S(6)} %select_n.10), kind=kOutput, calls=%fused_computation.23.clone.1 | convolution fusion | flops 679477248 | bytes 4763652 | tf_op jit(solution)/shard_map/while/body/eval_jaxpr/dot_general | solution.py:10
  138.2 1.1 multiply_reduce_fusion.6
  139.3 6.4 %fusion.46 = f32[32,512]{1,0:T(8,128)S(1)} fusion(f32[2048,512]{1,0:T(8,128)} %fusion.45, f32[2048]{0:T(1024)S(1)} %multiply_reduce_fusion.6, f32[512]{0:T(512)S(1)} %get-tuple-element.215, f32[32,16384]{1,0:T(8,128)} %get-tuple-element.214, s32[]{:T(128)S(6)} %select_n.10, f32[32,512]{1,0:T(8,128)S(1)} %get-tuple-element.203, pred[]{:T(512)S(6)} %compare.3), kind=kOutput, calls=%fused_computation.21.clone.1 | convolution fusion | flops 414220288 | bytes 4597765 | tf_op jit(solution)/shard_map/while/body/eval_jaxpr/dot_general | solution.py:23
  145.7 6.2 %fusion.45 = f32[2048,512]{1,0:T(8,128)} fusion(f32[54,512]{1,0:T(8,128)S(1)} %get-tuple-element.217, f32[54,16384]{1,0:T(8,128)} %get-tuple-element.216, s32[]{:T(128)S(6)} %select_n.10), kind=kOutput, calls=%fused_computation.23.clone.1 | convolution fusion | flops 679477248 | bytes 4763652 | tf_op jit(solution)/shard_map/while/body/eval_jaxpr/dot_general | solution.py:10
  151.9 1.1 multiply_reduce_fusion.6
  153.0 6.4 %fusion.46 = f32[32,512]{1,0:T(8,128)S(1)} fusion(f32[2048,512]{1,0:T(8,128)} %fusion.45, f32[2048]{0:T(1024)S(1)} %multiply_reduce_fusion.6, f32[512]{0:T(512)S(1)} %get-tuple-element.215, f32[32,16384]{1,0:T(8,128)} %get-tuple-element.214, s32[]{:T(128)S(6)} %select_n.10, f32[32,512]{1,0:T(8,128)S(1)} %get-tuple-element.203, pred[]{:T(512)S(6)} %compare.3), kind=kOutput, calls=%fused_computation.21.clone.1 | convolution fusion | flops 414220288 | bytes 4597765 | tf_op jit(solution)/shard_map/while/body/eval_jaxpr/dot_general | solution.py:23
  159.4 6.2 %fusion.45 = f32[2048,512]{1,0:T(8,128)} fusion(f32[54,512]{1,0:T(8,128)S(1)} %get-tuple-element.217, f32[54,16384]{1,0:T(8,128)} %get-tuple-element.216, s32[]{:T(128)S(6)} %select_n.10), kind=kOutput, calls=%fused_computation.23.clone.1 | convolution fusion | flops 679477248 | bytes 4763652 | tf_op jit(solution)/shard_map/while/body/eval_jaxpr/dot_general | solution.py:10
  165.6 1.1 multiply_reduce_fusion.6
  166.7 6.4 %fusion.46 = f32[32,512]{1,0:T(8,128)S(1)} fusion(f32[2048,512]{1,0:T(8,128)} %fusion.45, f32[2048]{0:T(1024)S(1)} %multiply_reduce_fusion.6, f32[512]{0:T(512)S(1)} %get-tuple-element.215, f32[32,16384]{1,0:T(8,128)} %get-tuple-element.214, s32[]{:T(128)S(6)} %select_n.10, f32[32,512]{1,0:T(8,128)S(1)} %get-tuple-element.203, pred[]{:T(512)S(6)} %compare.3), kind=kOutput, calls=%fused_computation.21.clone.1 | convolution fusion | flops 414220288 | bytes 4597765 | tf_op jit(solution)/shard_map/while/body/eval_jaxpr/dot_general | solution.py:23
  173.1 6.2 %fusion.45 = f32[2048,512]{1,0:T(8,128)} fusion(f32[54,512]{1,0:T(8,128)S(1)} %get-tuple-element.217, f32[54,16384]{1,0:T(8,128)} %get-tuple-element.216, s32[]{:T(128)S(6)} %select_n.10), kind=kOutput, calls=%fused_computation.23.clone.1 | convolution fusion | flops 679477248 | bytes 4763652 | tf_op jit(solution)/shard_map/while/body/eval_jaxpr/dot_general | solution.py:10
  179.3 1.1 multiply_reduce_fusion.6
  180.4 6.4 %fusion.46 = f32[32,512]{1,0:T(8,128)S(1)} fusion(f32[2048,512]{1,0:T(8,128)} %fusion.45, f32[2048]{0:T(1024)S(1)} %multiply_reduce_fusion.6, f32[512]{0:T(512)S(1)} %get-tuple-element.215, f32[32,16384]{1,0:T(8,128)} %get-tuple-element.214, s32[]{:T(128)S(6)} %select_n.10, f32[32,512]{1,0:T(8,128)S(1)} %get-tuple-element.203, pred[]{:T(512)S(6)} %compare.3), kind=kOutput, calls=%fused_computation.21.clone.1 | convolution fusion | flops 414220288 | bytes 4597765 | tf_op jit(solution)/shard_map/while/body/eval_jaxpr/dot_general | solution.py:23
  186.8 6.2 %fusion.45 = f32[2048,512]{1,0:T(8,128)} fusion(f32[54,512]{1,0:T(8,128)S(1)} %get-tuple-element.217, f32[54,16384]{1,0:T(8,128)} %get-tuple-element.216, s32[]{:T(128)S(6)} %select_n.10), kind=kOutput, calls=%fused_computation.23.clone.1 | convolution fusion | flops 679477248 | bytes 4763652 | tf_op jit(solution)/shard_map/while/body/eval_jaxpr/dot_general | solution.py:10
  193.0 1.1 multiply_reduce_fusion.6
  194.0 6.4 %fusion.46 = f32[32,512]{1,0:T(8,128)S(1)} fusion(f32[2048,512]{1,0:T(8,128)} %fusion.45, f32[2048]{0:T(1024)S(1)} %multiply_reduce_fusion.6, f32[512]{0:T(512)S(1)} %get-tuple-element.215, f32[32,16384]{1,0:T(8,128)} %get-tuple-element.214, s32[]{:T(128)S(6)} %select_n.10, f32[32,512]{1,0:T(8,128)S(1)} %get-tuple-element.203, pred[]{:T(512)S(6)} %compare.3), kind=kOutput, calls=%fused_computation.21.clone.1 | convolution fusion | flops 414220288 | bytes 4597765 | tf_op jit(solution)/shard_map/while/body/eval_jaxpr/dot_general | solution.py:23
  200.5 6.2 %fusion.45 = f32[2048,512]{1,0:T(8,128)} fusion(f32[54,512]{1,0:T(8,128)S(1)} %get-tuple-element.217, f32[54,16384]{1,0:T(8,128)} %get-tuple-element.216, s32[]{:T(128)S(6)} %select_n.10), kind=kOutput, calls=%fused_computation.23.clone.1 | convolution fusion | flops 679477248 | bytes 4763652 | tf_op jit(solution)/shard_map/while/body/eval_jaxpr/dot_general | solution.py:10
  206.7 1.1 multiply_reduce_fusion.6
  207.7 6.4 %fusion.46 = f32[32,512]{1,0:T(8,128)S(1)} fusion(f32[2048,512]{1,0:T(8,128)} %fusion.45, f32[2048]{0:T(1024)S(1)} %multiply_reduce_fusion.6, f32[512]{0:T(512)S(1)} %get-tuple-element.215, f32[32,16384]{1,0:T(8,128)} %get-tuple-element.214, s32[]{:T(128)S(6)} %select_n.10, f32[32,512]{1,0:T(8,128)S(1)} %get-tuple-element.203, pred[]{:T(512)S(6)} %compare.3), kind=kOutput, calls=%fused_computation.21.clone.1 | convolution fusion | flops 414220288 | bytes 4597765 | tf_op jit(solution)/shard_map/while/body/eval_jaxpr/dot_general | solution.py:23
  214.2 6.2 %fusion.45 = f32[2048,512]{1,0:T(8,128)} fusion(f32[54,512]{1,0:T(8,128)S(1)} %get-tuple-element.217, f32[54,16384]{1,0:T(8,128)} %get-tuple-element.216, s32[]{:T(128)S(6)} %select_n.10), kind=kOutput, calls=%fused_computation.23.clone.1 | convolution fusion | flops 679477248 | bytes 4763652 | tf_op jit(solution)/shard_map/while/body/eval_jaxpr/dot_general | solution.py:10
  220.4 1.1 multiply_reduce_fusion.6
  221.4 6.4 %fusion.46 = f32[32,512]{1,0:T(8,128)S(1)} fusion(f32[2048,512]{1,0:T(8,128)} %fusion.45, f32[2048]{0:T(1024)S(1)} %multiply_reduce_fusion.6, f32[512]{0:T(512)S(1)} %get-tuple-element.215, f32[32,16384]{1,0:T(8,128)} %get-tuple-element.214, s32[]{:T(128)S(6)} %select_n.10, f32[32,512]{1,0:T(8,128)S(1)} %get-tuple-element.203, pred[]{:T(512)S(6)} %compare.3), kind=kOutput, calls=%fused_computation.21.clone.1 | convolution fusion | flops 414220288 | bytes 4597765 | tf_op jit(solution)/shard_map/while/body/eval_jaxpr/dot_general | solution.py:23
  227.9 6.2 %fusion.45 = f32[2048,512]{1,0:T(8,128)} fusion(f32[54,512]{1,0:T(8,128)S(1)} %get-tuple-element.217, f32[54,16384]{1,0:T(8,128)} %get-tuple-element.216, s32[]{:T(128)S(6)} %select_n.10), kind=kOutput, calls=%fused_computation.23.clone.1 | convolution fusion | flops 679477248 | bytes 4763652 | tf_op jit(solution)/shard_map/while/body/eval_jaxpr/dot_general | solution.py:10
  234.0 1.1 multiply_reduce_fusion.6
  235.1 6.4 %fusion.46 = f32[32,512]{1,0:T(8,128)S(1)} fusion(f32[2048,512]{1,0:T(8,128)} %fusion.45, f32[2048]{0:T(1024)S(1)} %multiply_reduce_fusion.6, f32[512]{0:T(512)S(1)} %get-tuple-element.215, f32[32,16384]{1,0:T(8,128)} %get-tuple-element.214, s32[]{:T(128)S(6)} %select_n.10, f32[32,512]{1,0:T(8,128)S(1)} %get-tuple-element.203, pred[]{:T(512)S(6)} %compare.3), kind=kOutput, calls=%fused_computation.21.clone.1 | convolution fusion | flops 414220288 | bytes 4597765 | tf_op jit(solution)/shard_map/while/body/eval_jaxpr/dot_general | solution.py:23
  241.6 0.0 copy-done
  241.6 0.0 copy-done.1
  241.6 0.1 multiply_reduce_fusion.3
  241.7 38.9 %all-reduce = (f32[32]{0:T(128)S(1)}, f32[32]{0:T(128)S(1)}) all-reduce(f32[32]{0:T(128)S(1)} %get-tuple-element.154, f32[32]{0:T(128)S(1)} %get-tuple-element.153), channel_id=1, replica_groups=mesh['blk'=8,'grp'=4] {'blk','grp'}, use_global_device_ids=true, to_apply=%region_1.0 | all-reduce | flops 64 | bytes 512 | tf_op jit(solution)/shard_map/psum | solution.py:53
  280.6 0.0 copy-done.3
  280.6 0.8 multiply_reduce_fusion.2
  281.5 0.0 copy-start.2
  281.5 40.4 %psum.23 = f32[32]{0:T(128)S(1)} all-reduce(f32[32]{0:T(128)S(1)} %get-tuple-element.148), channel_id=1, replica_groups=mesh['blk'=8,'grp'=4] {'blk','grp'}, use_global_device_ids=true, to_apply=%region_9.0 | all-reduce | flops 32 | bytes 256 | tf_op jit(solution)/shard_map/psum | solution.py:69
  321.8 0.7 multiply_add_fusion
  322.6 0.0 copy-done.2
  (3 shorter events, 0.0 us)
Async XLA Ops:
  7.2 66.8 %all-gather.5.cloned.1.call-start = ((), (), s32[]{:S(2)}) async-start(), calls=%async_computation.1 | async-start | bytes 3784704 | tf_op jit(solution)/shard_map/all_gather | solution.py:54
  7.9 124.1 %all-gather.3.cloned.1.call-start = ((), (), s32[]{:S(2)}) async-start(), calls=%async_computation | async-start | bytes 2162688 | tf_op jit(solution)/shard_map/all_gather | solution.py:61
  132.0 109.6 %copy-start = (f32[32,512]{1,0:T(8,128)S(1)}, f32[32,512]{1,0:T(8,128)}, u32[]{:S(2)}) copy-start(f32[32,512]{1,0:T(8,128)} %param.13) | copy-start | bytes 196612
  132.0 109.6 %copy-start.1 = (f32[32,512]{1,0:T(8,128)S(1)}, f32[32,512]{1,0:T(8,128)}, u32[]{:S(2)}) copy-start(f32[32,512]{1,0:T(8,128)} %param.12) | copy-start | bytes 196612
  132.0 148.6 %copy-start.3 = (f32[32,512]{1,0:T(8,128)S(1)}, f32[32,512]{1,0:T(8,128)}, u32[]{:S(2)}) copy-start(f32[32,512]{1,0:T(8,128)} %param.11) | copy-start | bytes 196612
  281.5 41.1 %copy-start.2 = (f32[32,512]{1,0:T(8,128)}, f32[32,512]{1,0:T(8,128)S(1)}, u32[]{:S(2)}) copy-start(f32[32,512]{1,0:T(8,128)S(1)} %get-tuple-element.149) | copy-start | bytes 196612
Sparse Core Ops, SparseCore 0:
  11.0 62.9 all-gather.4
  77.0 54.9 all-gather.2
where the time goes:
time: 330 us; the launch traced here: 329 us
  waiting for transfers between devices  119 us (36%)
  matrix products  101 us (31%)
  blocking collectives  79.3 us (24%)
  other arithmetic  15.4 us (5%)
  between operations  14.7 us (4%)
    all_gather x1, waiting for transfers between devices, per_device(): lax.all_gather(states, ('blk', 'grp'), axis=1, tiled=True) - 0.5  63.7 us
    all_gather x1, waiting for transfers between devices, per_device(): lax.all_gather(direction, ('blk', 'grp'), axis=1, tiled=True)  53.8 us
    dot_general x8, matrix products, apply_kernel(): lax.dot_general(batch_descent_vectors, kernel, (((1,), (1,)), ((), ())),...  51.4 us
    dot_general x8, matrix products, matern_tile(): jnp.dot(rows_scaled.T, cols_scaled, precision=lax.Precision.HIGHEST, pref...  49.4 us
    psum x1, blocking collectives, per_device(): lax.psum(jnp.sum(new_residual * new_residual, axis=1), ('blk', 'grp'))  40.4 us
    psum x1, blocking collectives, per_device(): old_norm = lax.psum(local_norm, ('blk', 'grp'))  38.9 us
    reduce_sum x8, other arithmetic, matern_tile(): column_norm_value = jnp.sum(cols_scaled * cols_scaled, axis=0)  8.56 us
  transfers between devices with their start and end apart: 2, of which 2 were waited for; matrix products, arithmetic and copies ran while one was open for 2% of the time, Pallas kernels for 0%

commit v1 on v0

v1 whole, which is shorter than its diff:
```python
import functools
import math

import jax
import jax.numpy as jnp
from jax import lax
from jax.experimental import pallas as pl
from jax.experimental.pallas import tpu as pltpu
from jax.sharding import PartitionSpec as P

MESH = pl.DeviceIdType.MESH
F32 = jnp.float32
BF16 = jnp.bfloat16
TO_T = math.sqrt(5.0) / math.log(2.0)
LN2 = math.log(2.0)


def partner(index, flip, count):
    bit = 1
    while bit < count:
        if not isinstance(flip, int):
            turn = lax.rem(lax.div(flip, bit), 2)
            index = index + turn * bit * (1 - 2 * lax.rem(lax.div(index, bit), 2))
        elif flip & bit:
            index = index + bit * (1 - 2 * lax.rem(lax.div(index, bit), 2))
        bit *= 2
    return index


def step_order(pairs, groups):
    order = [(p, r) for p in range(pairs - 1) for r in range(groups)]
    order.sort(key=lambda s: (max(s), s[0], s[1]))
    return order + [(pairs - 1, r) for r in reversed(range(groups))]


def split(x):
    high = x.astype(BF16).astype(F32)
    return high, (x - high).astype(BF16).astype(F32)


def norm_terms(high, low):
    both = high + low
    norm = jnp.sum(both * both, axis=0, keepdims=True)
    n1, rest = split(norm)
    n2 = rest
    n3 = (norm - n1 - n2).astype(BF16).astype(F32)
    return n1, n2, n3


def stacked(blocks, norms, first):
    width = blocks[0].shape[1]
    n1, n2, n3 = norms
    row = lax.broadcasted_iota(jnp.int32, (8, width), 0)
    at = first
    other = 3 - first
    extra = jnp.where((row >= other) & (row < other + 3), 1.0, 0.0)
    extra = jnp.where(row == at, n1, extra)
    extra = jnp.where(row == at + 1, n2, extra)
    extra = jnp.where(row == at + 2, n3, extra)
    used = sum(b.shape[0] for b in blocks) + 8
    depth = -(-used // 256) * 256
    parts = list(blocks) + [extra]
    if depth > used:
        parts.append(jnp.zeros((depth - used, width), F32))
    return jnp.concatenate(parts, axis=0)


def matern(x):
    x = jnp.maximum(x, 1e-30)
    t = x * lax.rsqrt(x)
    k = (x * (LN2 * LN2 / 3.0) + 1.0 + t * LN2) * jnp.exp2(-t)
    high = k.astype(BF16)
    return high, (k - high.astype(F32)).astype(BF16)


def kernel(
    nb, ng, dims, padded, st_ref, ls_ref, nv_ref, sol_ref, res_ref, dir_ref,
    nsol_ref, nres_ref, ndir_ref,
    colbuf, rowbuf, acol, brow, dd, acc, outbuf, redbuf, sums1, sums2,
    csend, crecv, fsend, frecv, rsend, rrecv, isend, irecv, s1send, s1recv, s2send, s2recv,
):
    b = lax.axis_index("blk")
    g = lax.axis_index("grp")
    pairs = nb // 2
    probes, n = dir_ref.shape
    q, core = lax.div(b, 2), lax.rem(b, 2)
    sibling = q * 2 + (1 - core)

    barrier = pltpu.get_barrier_semaphore()
    for k in range(1, nb):
        pl.semaphore_signal(barrier, inc=1, device_id=(partner(b, k, nb), g), device_id_type=MESH)
    for k in range(1, ng):
        pl.semaphore_signal(barrier, inc=1, device_id=(b, partner(g, k, ng)), device_id_type=MESH)

    colbuf[0, 0, padded - 8 : padded, :] = jnp.zeros((8, n), F32)
    colbuf[0, 0, 0:dims, :] = (st_ref[...] - 0.5) / ls_ref[...] * TO_T
    colbuf[0, 0, padded:, :] = dir_ref[...]
    acc[...] = jnp.zeros_like(acc)
    pl.semaphore_wait(barrier, nb + ng - 2)

    def direct(p):
        to = sibling if p is None else partner(q, p, pairs) * 2 + core
        slot = (0, 1) if p is None else (p, 0)
        at = 0 if p is None else p
        return pltpu.make_async_remote_copy(
            src_ref=colbuf.at[0, 0], dst_ref=colbuf.at[slot[0], slot[1]],
            send_sem=csend.at[at], recv_sem=crecv.at[at],
            device_id=(to, g), device_id_type=MESH,
        )

    def forward(p):
        return pltpu.make_async_remote_copy(
            src_ref=colbuf.at[p, 0], dst_ref=colbuf.at[p, 1],
            send_sem=fsend.at[p], recv_sem=frecv.at[p],
            device_id=(sibling, g), device_id_type=MESH,
        )

    def arrival(src, dst, sem):
        pltpu.make_async_copy(src, dst, sem).wait()

    def row_copy(r):
        return pltpu.make_async_remote_copy(
            src_ref=colbuf.at[0, 0, pl.ds(0, padded)], dst_ref=rowbuf.at[r],
            send_sem=rsend.at[r], recv_sem=rrecv.at[r],
            device_id=(b, partner(g, r, ng)), device_id_type=MESH,
        )

    def image_copy(r):
        return pltpu.make_async_remote_copy(
            src_ref=outbuf.at[r], dst_ref=redbuf.at[r],
            send_sem=isend.at[r], recv_sem=irecv.at[r],
            device_id=(b, partner(g, r, ng)), device_id_type=MESH,
        )

    direct(None).start()
    for k in range(1, max(pairs, ng)):
        if k < ng:
            row_copy(k).start()
        if k < pairs:
            direct(k).start()

    def prepare_rows(r, src):
        high, low = split(src)
        brow[r] = stacked([high, low, high, low], norm_terms(high, low), 3).astype(BF16)

    def prepare_columns(p, half):
        high, low = split(colbuf[p, half, 0:padded, :])
        left = stacked([-2.0 * high, -2.0 * high, -2.0 * low, -2.0 * low], norm_terms(high, low), 0)
        acol[p, half * n : (half + 1) * n, :] = left.T.astype(BF16)
        d1, d2 = split(colbuf[p, half, padded:, :])
        both = jnp.concatenate([d1, d2], axis=0).astype(BF16)
        dd[p, :, half * n : (half + 1) * n] = both
        dd[p, :, (2 + half) * n : (3 + half) * n] = both

    prepare_rows(0, colbuf[0, 0, 0:padded, :])

    order = step_order(pairs, ng)
    first_p, first_r, last_r = {}, {}, {}
    for s, (p, r) in enumerate(order):
        first_p.setdefault(p, s)
        first_r.setdefault(r, s)
        last_r[r] = s
    ahead = {}
    for p in range(1, pairs):
        s = max(first_p[p] - (1 if p == 1 else 2), 0)
        while s in ahead:
            s -= 1
        ahead[s] = p
    codes = []
    for s, (p, r) in enumerate(order):
        flags = (first_p[p] == s) + 2 * (first_r[r] == s and r > 0) + 4 * (last_r[r] == s and r > 0)
        codes.append(((ahead.get(s, 0) * 8 + flags) * ng + r) * pairs + p)

    def one_step(s, carry):
        code = jnp.int32(codes[0])
        for k in range(1, len(codes)):
            code = jnp.where(s == k, jnp.int32(codes[k]), code)
        p = lax.rem(code, pairs)
        r = lax.rem(lax.div(code, pairs), ng)
        flags = lax.rem(lax.div(code, pairs * ng), 8)
        early = lax.div(code, pairs * ng * 8)

        @pl.when(early > 0)
        def _():
            arrival(colbuf.at[0, 0], colbuf.at[early, 0], crecv.at[early])
            forward(early).start()

        @pl.when(lax.rem(flags, 2) == 1)
        def _():
            prepare_columns(p, 0)

            @pl.when(p == 0)
            def _():
                arrival(colbuf.at[0, 0], colbuf.at[0, 1], crecv.at[0])

            @pl.when(p > 0)
            def _():
                arrival(colbuf.at[0, 0], colbuf.at[p, 1], frecv.at[p])

            prepare_columns(p, 1)

        @pl.when(lax.rem(lax.div(flags, 2), 2) == 1)
        def _():
            arrival(colbuf.at[0, 0, pl.ds(0, padded)], rowbuf.at[r], rrecv.at[r])
            prepare_rows(r, rowbuf[r])

        x = jnp.dot(acol[p], brow[r], preferred_element_type=F32)
        high, low = matern(x)
        acc[r] += jnp.dot(dd[p], jnp.concatenate([high, low], axis=0), preferred_element_type=F32)

        @pl.when(flags >= 4)
        def _():
            outbuf[r] = acc[r, 0:probes, :] + acc[r, probes:, :]
            image_copy(r).start()

        return carry

    lax.fori_loop(0, len(codes), one_step, 0)

    direction = dir_ref[...]
    residual = res_ref[...]
    image = acc[0, 0:probes, :] + acc[0, probes:, :]
    for r in reversed(range(1, ng)):
        image_copy(r).wait_recv()
        image = image + redbuf[r]
    image = image + nv_ref[0, 0] * direction

    lane = lax.broadcasted_iota(jnp.int32, (128, 128), 1)
    gathered = jnp.zeros((128, 128), F32)
    for k, (u, v) in enumerate(
        [(residual, residual), (direction, image), (residual, image), (image, image)]
    ):
        one = jnp.sum(u * v, axis=1, keepdims=True)
        one = jnp.concatenate([one, jnp.zeros((128 - probes, 1), F32)], axis=0)
        gathered = jnp.where(lane == k, one, gathered)
    sums1[0] = gathered.T[0:8, :]

    def sums_copy(k, buf, send, recv, to):
        return pltpu.make_async_remote_copy(
            src_ref=buf.at[0], dst_ref=buf.at[k], send_sem=send.at[k], recv_sem=recv.at[k],
            device_id=to, device_id_type=MESH,
        )

    for k in range(1, nb):
        sums_copy(k, sums1, s1send, s1recv, (partner(b, k, nb), g)).start()
    total = sums1[0]
    for k in range(1, nb):
        sums_copy(k, sums1, s1send, s1recv, (partner(b, k, nb), g)).wait_recv()
        total = total + sums1[k]
    sums2[0] = total
    for k in range(1, ng):
        sums_copy(k, sums2, s2send, s2recv, (b, partner(g, k, ng))).start()
    for k in range(1, ng):
        sums_copy(k, sums2, s2send, s2recv, (b, partner(g, k, ng))).wait_recv()
        total = total + sums2[k]
    columns = jnp.concatenate([total, jnp.zeros((120, 128), F32)], axis=0).T
    rr, curv, ri, ii = [columns[0:probes, k : k + 1] for k in range(4)]
    alpha = rr / curv
    fresh = rr - 2.0 * alpha * ri + alpha * alpha * ii
    beta = fresh / rr
    nsol_ref[...] = sol_ref[...] + alpha * direction
    new_residual = residual - alpha * image
    nres_ref[...] = new_residual
    ndir_ref[...] = new_residual + beta * direction

    direct(None).wait_send()
    for k in range(1, pairs):
        direct(k).wait_send()
        forward(k).wait_send()
    for k in range(1, ng):
        row_copy(k).wait_send()
        image_copy(k).wait_send()
        sums_copy(k, sums2, s2send, s2recv, (b, partner(g, k, ng))).wait_send()
    for k in range(1, nb):
        sums_copy(k, sums1, s1send, s1recv, (partner(b, k, nb), g)).wait_send()


def solution(mesh):
    nb, ng = mesh.shape["blk"], mesh.shape["grp"]

    def per_device(states, lengthscales, noise_var, solution, residual, direction):
        dims, n = states.shape
        probes = direction.shape[0]
        padded = -(-dims // 8) * 8
        pairs = nb // 2
        depth = -(-(4 * padded + 8) // 256) * 256
        vmem = pl.BlockSpec(memory_space=pltpu.VMEM)
        smem = pl.BlockSpec(memory_space=pltpu.SMEM)
        dma = pltpu.SemaphoreType.DMA
        out = jax.ShapeDtypeStruct((probes, n), F32)
        return pl.pallas_call(
            functools.partial(kernel, nb, ng, dims, padded),
            out_shape=(out, out, out),
            in_specs=[vmem, vmem, smem, vmem, vmem, vmem],
            out_specs=(vmem, vmem, vmem),
            scratch_shapes=[
                pltpu.VMEM((pairs, 2, padded + probes, n), F32),
                pltpu.VMEM((ng, padded, n), F32),
                pltpu.VMEM((pairs, 2 * n, depth), BF16),
                pltpu.VMEM((ng, depth, n), BF16),
                pltpu.VMEM((pairs, 2 * probes, 4 * n), BF16),
                pltpu.VMEM((ng, 2 * probes, n), F32),
                pltpu.VMEM((ng, probes, n), F32),
                pltpu.VMEM((ng, probes, n), F32),
                pltpu.VMEM((nb, 8, 128), F32),
                pltpu.VMEM((ng, 8, 128), F32),
                dma((pairs,)), dma((pairs,)), dma((pairs,)), dma((pairs,)),
                dma((ng,)), dma((ng,)), dma((ng,)), dma((ng,)),
                dma((nb,)), dma((nb,)), dma((ng,)), dma((ng,)),
            ],
            compiler_params=pltpu.CompilerParams(
                collective_id=0, has_side_effects=True, vmem_limit_bytes=56 * 2**20
            ),
        )(states, lengthscales[:, None], noise_var[:, None], solution, residual, direction)

    spec = P(None, ("blk", "grp"))
    return jax.shard_map(
        per_device,
        mesh=mesh,
        in_specs=(spec, P(), P(), spec, spec, spec),
        out_specs=(spec, spec, spec),
        check_vma=False,
    )
```

time: 330 us -> 51.6 us (0.16)
  waiting for transfers between devices: 119 us -> 0 us
  matrix products: 101 us -> 0 us
  blocking collectives: 79.3 us -> 0 us
  Pallas kernels: 0 us -> 45.7 us
  other arithmetic: 15.4 us -> 0 us
  between operations: 14.7 us -> 1.3 us
  local copies, waits for them, and re-layouts: 0.01 us -> 4.36 us
    all_gather x2 -> x0, waiting for transfers between devices: 117 us -> none  [the longest x1 63.7 us: per_device(): lax.all_gather(states, ('blk', 'grp'), axis=1, tiled=True) - 0.5]
    dot_general x16 -> x0, matrix products: 101 us -> none  [the longest x8 51.4 us: apply_kernel(): lax.dot_general(batch_descent_vectors, kernel, (((1,), (1,)), ((), ())),...]
    psum x2 -> x0, blocking collectives: 79.3 us -> none  [the longest x1 40.4 us: per_device(): lax.psum(jnp.sum(new_residual * new_residual, axis=1), ('blk', 'grp'))]
    pallas_call x0 -> x1, Pallas kernels: none -> 45.7 us  [per_device(): pl.pallas_call(functools.partial(kernel, nb, ng, dims, padded), out_shape...]
    reduce_sum x11 -> x0, other arithmetic: 10.5 us -> none  [the longest x8 8.56 us: matern_tile(): column_norm_value = jnp.sum(cols_scaled * cols_scaled, axis=0)]
    div x3 -> x0, other arithmetic: 4.2 us -> none  [the longest x1 4.2 us: per_device(): (lax.all_gather(states, ('blk', 'grp'), axis=1, tiled=True) - 0.5) / leng...]
    unnamed x8 -> x9, local copies, waits for them, and re-layouts: 0.01 us -> 3.65 us
  transfers between devices with their start and end apart: 2 -> 0, of which waited for: 2 -> 0; matrix products, arithmetic and copies ran while one was open for 2% -> 0% of each run, Pallas kernels for 0% -> 0%
where the time goes in v1:
time: 51.6 us; the launch traced here: 51.3 us
  Pallas kernels  45.7 us (89%)
  local copies, waits for them, and re-layouts  4.36 us (8%)
  between operations  1.3 us (3%)
    pallas_call x1, Pallas kernels, per_device(): pl.pallas_call(functools.partial(kernel, nb, ng, dims, padded), out_shape...  45.7 us
    unnamed x9, local copies, waits for them, and re-layouts  3.65 us

profile of v1, /device:TPU:0, one launch (start us, length us, event | category | flops | bytes accessed | tf_op | source)
XLA Modules:
  0.0 51.3 jit_solution(7755502454031618194)
XLA Ops:
  1.3 0.0 copy-start.2
  1.3 0.6 %copy-done.2 = f32[54]{0:T(128)S(1)} copy-done((f32[54]{0:T(128)S(1)}, f32[54]{0:T(128)}, u32[]{:S(2)}) %copy-start.2) | copy-done | bytes 240
  1.9 0.7 %copy.9.ls_ref = f32[54,1]{1,0:T(8,128)} copy(f32[54,1]{0,1:T(1,128)S(1)} %bitcast.3) | data formatting | bytes 432 | tf_op jit(solution)/shard_map/broadcast_in_dim | solution.py:314
  2.6 45.7 %shard_map.85 = (f32[32,512]{1,0:T(8,128)}, f32[32,512]{1,0:T(8,128)}, f32[32,512]{1,0:T(8,128)}) custom-call(f32[54,512]{1,0:T(8,128)} %st_ref.1, f32[54,1]{1,0:T(8,128)} %copy.9.ls_ref, f32[1,1]{1,0:T(1,128)} %bitcast.2.nv_ref, f32[32,512]{1,0:T(8,128)} %sol_ref.1, f32[32,512]{1,0:T(8,128)} %res_ref.1, f32[32,512]{1,0:T(8,128)} %dir_ref.1), custom_call_target="tpu_custom_call" | custom-call | tf_op jit(solution)/shard_map/pallas_call | solution.py:291
  48.3 0.0 copy-start.1
  48.3 1.5 %copy.14 = f32[32,512]{1,0:T(8,128)} copy(f32[32,512]{1,0:T(8,128)} %get-tuple-element.6) | data formatting | bytes 131072
  49.8 0.0 copy-done.1
  49.8 0.0 copy-start
  49.8 0.6 %copy.15 = f32[32,512]{1,0:T(8,128)} copy(f32[32,512]{1,0:T(8,128)S(1)} %copy-done.1) | data formatting | bytes 131072
  50.5 0.2 copy-done
  50.7 0.6 %copy.16 = f32[32,512]{1,0:T(8,128)} copy(f32[32,512]{1,0:T(8,128)S(1)} %copy-done) | data formatting | bytes 131072
Async XLA Ops:
  1.3 0.7 %copy-start.2 = (f32[54]{0:T(128)S(1)}, f32[54]{0:T(128)}, u32[]{:S(2)}) copy-start(f32[54]{0:T(128)} %param.7) | copy-start | bytes 652
  48.3 1.5 %copy-start.1 = (f32[32,512]{1,0:T(8,128)S(1)}, f32[32,512]{1,0:T(8,128)}, u32[]{:S(2)}) copy-start(f32[32,512]{1,0:T(8,128)} %get-tuple-element.7) | copy-start | bytes 196612
  49.8 0.9 %copy-start = (f32[32,512]{1,0:T(8,128)S(1)}, f32[32,512]{1,0:T(8,128)}, u32[]{:S(2)}) copy-start(f32[32,512]{1,0:T(8,128)} %get-tuple-element.8) | copy-start | bytes 196612

commit v2 on v1

v2 whole, which is shorter than its diff:
```python
import functools
import math

import jax
import jax.numpy as jnp
from jax import lax
from jax.experimental import pallas as pl
from jax.experimental.pallas import tpu as pltpu
from jax.sharding import PartitionSpec as P

MESH = pl.DeviceIdType.MESH
F32 = jnp.float32
BF16 = jnp.bfloat16
TO_T = math.sqrt(5.0) / math.log(2.0)
LN2 = math.log(2.0)


def partner(index, flip, count):
    bit = 1
    while bit < count:
        if not isinstance(flip, int):
            turn = lax.rem(lax.div(flip, bit), 2)
            index = index + turn * bit * (1 - 2 * lax.rem(lax.div(index, bit), 2))
        elif flip & bit:
            index = index + bit * (1 - 2 * lax.rem(lax.div(index, bit), 2))
        bit *= 2
    return index


def step_order(pairs, groups):
    tail = [(p, 0) for p in range(max(pairs - 2, 1), pairs)]
    order = [(p, r) for p in range(pairs) for r in range(groups) if (p, r) not in tail]
    order.sort(key=lambda s: (max(2 * s[0], 4 * s[1] - 3), s[1], s[0]))
    return order + tail


def split(x):
    high = x.astype(BF16).astype(F32)
    return high, (x - high).astype(BF16).astype(F32)


def norm_terms(high, low):
    both = high + low
    norm = jnp.sum(both * both, axis=0, keepdims=True)
    n1, rest = split(norm)
    n2 = rest
    n3 = (norm - n1 - n2).astype(BF16).astype(F32)
    return n1, n2, n3


def stacked(blocks, norms, first):
    width = blocks[0].shape[1]
    n1, n2, n3 = norms
    row = lax.broadcasted_iota(jnp.int32, (8, width), 0)
    at = first
    other = 3 - first
    extra = jnp.where((row >= other) & (row < other + 3), 1.0, 0.0)
    extra = jnp.where(row == at, n1, extra)
    extra = jnp.where(row == at + 1, n2, extra)
    extra = jnp.where(row == at + 2, n3, extra)
    used = sum(b.shape[0] for b in blocks) + 8
    depth = -(-used // 256) * 256
    parts = list(blocks) + [extra]
    if depth > used:
        parts.append(jnp.zeros((depth - used, width), F32))
    return jnp.concatenate(parts, axis=0)


def matern(x):
    x = jnp.maximum(x, 1e-30)
    t = x * lax.rsqrt(x)
    k = (x * (LN2 * LN2 / 3.0) + 1.0 + t * LN2) * jnp.exp2(-t)
    high = k.astype(BF16)
    return high, (k - high.astype(F32)).astype(BF16)


def kernel(
    nb, ng, dims, padded, st_ref, ls_ref, nv_ref, res_ref, dir_ref,
    image_ref, steps_ref,
    colbuf, rowbuf, acol, brow, dd, acc, outbuf, redbuf, sums, xbuf,
    csend, crecv, fsend, frecv, rsend, rrecv, isend, irecv, ssend, srecv,
):
    b = lax.axis_index("blk")
    g = lax.axis_index("grp")
    pairs = nb // 2
    probes, n = dir_ref.shape
    q, core = lax.div(b, 2), lax.rem(b, 2)
    sibling = q * 2 + (1 - core)

    others = [(i, j) for i in range(nb) for j in range(ng) if i + j > 0]

    def other(i, j):
        return partner(b, i, nb), partner(g, j, ng)

    barrier = pltpu.get_barrier_semaphore()
    for i, j in others:
        pl.semaphore_signal(barrier, inc=1, device_id=other(i, j), device_id_type=MESH)

    diagonal = lax.broadcasted_iota(jnp.int32, (dims, dims), 0) == lax.broadcasted_iota(
        jnp.int32, (dims, dims), 1
    )
    lengths = jnp.sum(jnp.where(diagonal, ls_ref[...], 0.0), axis=1, keepdims=True)
    colbuf[0, 0, padded - 8 : padded, :] = jnp.zeros((8, n), F32)
    colbuf[0, 0, 0:dims, :] = (st_ref[...] - 0.5) / lengths * TO_T
    colbuf[0, 0, padded:, :] = dir_ref[...]
    acc[...] = jnp.zeros_like(acc)
    pl.semaphore_wait(barrier, len(others))

    def direct(p):
        to = sibling if p is None else partner(q, p, pairs) * 2 + core
        slot = (0, 1) if p is None else (p, 0)
        at = 0 if p is None else p
        return pltpu.make_async_remote_copy(
            src_ref=colbuf.at[0, 0], dst_ref=colbuf.at[slot[0], slot[1]],
            send_sem=csend.at[at], recv_sem=crecv.at[at],
            device_id=(to, g), device_id_type=MESH,
        )

    def forward(p):
        return pltpu.make_async_remote_copy(
            src_ref=colbuf.at[p, 0], dst_ref=colbuf.at[p, 1],
            send_sem=fsend.at[p], recv_sem=frecv.at[p],
            device_id=(sibling, g), device_id_type=MESH,
        )

    def arrival(src, dst, sem):
        pltpu.make_async_copy(src, dst, sem).wait()

    def row_copy(r):
        return pltpu.make_async_remote_copy(
            src_ref=colbuf.at[0, 0, pl.ds(0, padded)], dst_ref=rowbuf.at[r],
            send_sem=rsend.at[r], recv_sem=rrecv.at[r],
            device_id=(b, partner(g, r, ng)), device_id_type=MESH,
        )

    def image_copy(r):
        return pltpu.make_async_remote_copy(
            src_ref=outbuf.at[r], dst_ref=redbuf.at[r],
            send_sem=isend.at[r], recv_sem=irecv.at[r],
            device_id=(b, partner(g, r, ng)), device_id_type=MESH,
        )

    direct(None).start()
    if ng > 1:
        row_copy(1).start()
    for p in range(1, min(pairs, 3)):
        direct(p).start()

    def prepare_rows(r, src):
        high, low = split(src)
        brow[r] = stacked([high, low, high, low], norm_terms(high, low), 3).astype(BF16)

    def prepare_columns(p, half):
        high, low = split(colbuf[p, half, 0:padded, :])
        left = stacked([-2.0 * high, -2.0 * high, -2.0 * low, -2.0 * low], norm_terms(high, low), 0)
        acol[p, half * n : (half + 1) * n, :] = left.T.astype(BF16)
        d1, d2 = split(colbuf[p, half, padded:, :])
        both = jnp.concatenate([d1, d2], axis=0).astype(BF16)
        dd[p, :, half * n : (half + 1) * n] = both
        dd[p, :, (2 + half) * n : (3 + half) * n] = both

    order = step_order(pairs, ng)
    count = len(order)
    first_p, first_r, last_r = {}, {}, {}
    for s, (p, r) in enumerate(order):
        first_p.setdefault(p, s)
        first_r.setdefault(r, s)
        last_r[r] = s
    ahead = {}
    for p in range(3, pairs):
        s = first_p[p] - 2
        while s in ahead:
            s -= 1
        ahead[s] = p
    codes = []
    for s, (p, r) in enumerate(order):
        flags = (first_p[p] == s) + 2 * (first_r[r] == s) + 4 * (last_r[r] == s and r > 0)
        codes.append(((ahead.get(s, 0) * 8 + flags) * ng + r) * pairs + p)

    def decode(s):
        code = jnp.int32(codes[0])
        for k in range(1, count):
            code = jnp.where(s == k, jnp.int32(codes[k]), code)
        group = lax.div(code, pairs)
        flags = lax.div(group, ng)
        return lax.rem(code, pairs), lax.rem(group, ng), lax.rem(flags, 8), lax.div(flags, 8)

    def pass_on(p):
        arrival(colbuf.at[0, 0], colbuf.at[p, 0], crecv.at[p])
        forward(p).start()

    def rows_arrive(r):
        arrival(colbuf.at[0, 0, pl.ds(0, padded)], rowbuf.at[r], rrecv.at[r])
        prepare_rows(r, rowbuf[r])

    def columns_arrive(p):
        prepare_columns(p, 0)
        arrival(colbuf.at[0, 0], colbuf.at[p, 1], frecv.at[p])
        prepare_columns(p, 1)

    def get_ready(s):
        p, r, flags, early = decode(s)

        @pl.when(early > 0)
        def _():
            pass_on(early)

        @pl.when(lax.rem(flags, 2) == 1)
        def _():
            columns_arrive(p)

        @pl.when(lax.rem(lax.div(flags, 2), 2) == 1)
        def _():
            rows_arrive(r)

    def distance(p, r):
        return jnp.dot(acol[p], brow[r], preferred_element_type=F32)

    def accumulate(p, r, x):
        high, low = matern(x)
        acc[r] += jnp.dot(dd[p], jnp.concatenate([high, low], axis=0), preferred_element_type=F32)

    def send_off(r, flags):
        @pl.when(flags >= 4)
        def _():
            outbuf[r] = acc[r, 0:probes, :] + acc[r, probes:, :]
            image_copy(r).start()

    prepare_columns(0, 0)
    prepare_rows(0, colbuf[0, 0, 0:padded, :])
    arrival(colbuf.at[0, 0], colbuf.at[0, 1], crecv.at[0])
    prepare_columns(0, 1)
    xbuf[0] = distance(0, 0)
    seen = {("p", 0), ("r", 0)}
    for s in range(1, 3):
        p, r = order[s]
        if ("r", r) not in seen:
            rows_arrive(r)
            if r + 1 < ng:
                row_copy(r + 1).start()
        if ("p", p) not in seen:
            for k in range(1, min(pairs, 3)):
                pass_on(k)
            if pairs > 3:
                direct(3).start()
            columns_arrive(p)
        seen |= {("p", p), ("r", r)}

    def two_steps(i, carry):
        s = 2 * i
        p0, r0, flags0, _ = decode(s)
        p1, r1, flags1, _ = decode(s + 1)
        p2, r2, _, _ = decode(s + 2)
        xbuf[1] = distance(p1, r1)
        accumulate(p0, r0, xbuf[0])
        xbuf[0] = distance(p2, r2)
        accumulate(p1, r1, xbuf[1])
        send_off(r0, flags0)
        send_off(r1, flags1)
        for first, total, copy in ((3, ng, row_copy), (4, pairs, direct)):
            if first < total:

                @pl.when(i + first < total)
                def _():
                    copy(i + first).start()

        def ready(k, carry):
            get_ready(s + 3 + k)
            return carry

        lax.fori_loop(0, jnp.minimum(2, count - 3 - s), ready, 0)
        return carry

    lax.fori_loop(0, count // 2 - 1, two_steps, 0)
    (p0, r0), (p1, r1) = order[-2:]
    xbuf[1] = distance(p1, r1)
    accumulate(p0, r0, xbuf[0])
    accumulate(p1, r1, xbuf[1])

    direction = dir_ref[...]
    residual = res_ref[...]
    image = acc[0, 0:probes, :] + acc[0, probes:, :]
    for r in reversed(range(1, ng)):
        image_copy(r).wait_recv()
        image = image + redbuf[r]
    image = image + nv_ref[0, 0] * direction

    products = [residual * residual, direction * image, residual * image, image * image]
    columns = jnp.concatenate([jnp.sum(u, axis=1, keepdims=True) for u in products], axis=0)
    sums[0] = jnp.broadcast_to(columns, (4 * probes, 128)).T[0:1, :]

    def sums_copy(i, j):
        slot = i * ng + j
        return pltpu.make_async_remote_copy(
            src_ref=sums.at[0], dst_ref=sums.at[slot], send_sem=ssend.at[slot], recv_sem=srecv.at[slot],
            device_id=other(i, j), device_id_type=MESH,
        )

    for i, j in others:
        sums_copy(i, j).start()
    image_ref[...] = image
    for i, j in others:
        sums_copy(i, j).wait_recv()
    total = jnp.sum(sums[...], axis=0)
    totals = jnp.broadcast_to(total, (128, 4 * probes)).T
    rr, curv, ri, ii = [totals[k * probes : (k + 1) * probes, :] for k in range(4)]
    alpha = rr / curv
    fresh = rr - 2.0 * alpha * ri + alpha * alpha * ii
    steps_ref[0] = alpha
    steps_ref[1] = fresh / rr

    direct(None).wait_send()
    for k in range(1, pairs):
        direct(k).wait_send()
        forward(k).wait_send()
    for k in range(1, ng):
        row_copy(k).wait_send()
        image_copy(k).wait_send()
    for i, j in others:
        sums_copy(i, j).wait_send()


def solution(mesh):
    nb, ng = mesh.shape["blk"], mesh.shape["grp"]

    def per_device(states, lengthscales, noise_var, solution, residual, direction):
        dims, n = states.shape
        probes = direction.shape[0]
        padded = -(-dims // 8) * 8
        pairs = nb // 2
        depth = -(-(4 * padded + 8) // 256) * 256
        vmem = pl.BlockSpec(memory_space=pltpu.VMEM)
        smem = pl.BlockSpec(memory_space=pltpu.SMEM)
        dma = pltpu.SemaphoreType.DMA
        image, steps = pl.pallas_call(
            functools.partial(kernel, nb, ng, dims, padded),
            out_shape=(
                jax.ShapeDtypeStruct((probes, n), F32),
                jax.ShapeDtypeStruct((2, probes, 128), F32),
            ),
            in_specs=[vmem, vmem, smem, vmem, vmem],
            out_specs=(vmem, vmem),
            scratch_shapes=[
                pltpu.VMEM((pairs, 2, padded + probes, n), F32),
                pltpu.VMEM((ng, padded, n), F32),
                pltpu.VMEM((pairs, 2 * n, depth), BF16),
                pltpu.VMEM((ng, depth, n), BF16),
                pltpu.VMEM((pairs, 2 * probes, 4 * n), BF16),
                pltpu.VMEM((ng, 2 * probes, n), F32),
                pltpu.VMEM((ng, probes, n), F32),
                pltpu.VMEM((ng, probes, n), F32),
                pltpu.VMEM((nb * ng, 1, 4 * probes), F32),
                pltpu.VMEM((2, 2 * n, n), F32),
                dma((pairs,)), dma((pairs,)), dma((pairs,)), dma((pairs,)),
                dma((ng,)), dma((ng,)), dma((ng,)), dma((ng,)),
                dma((nb * ng,)), dma((nb * ng,)),
            ],
            compiler_params=pltpu.CompilerParams(
                collective_id=0, has_side_effects=True, vmem_limit_bytes=56 * 2**20
            ),
        )(states, lengthscales[None, :], noise_var[:, None], residual, direction)
        alpha, beta = steps[0, :, 0:1], steps[1, :, 0:1]
        new_residual = residual - alpha * image
        return solution + alpha * direction, new_residual, new_residual + beta * direction

    spec = P(None, ("blk", "grp"))
    return jax.shard_map(
        per_device,
        mesh=mesh,
        in_specs=(spec, P(), P(), spec, spec, spec),
        out_specs=(spec, spec, spec),
        check_vma=False,
    )
```

time: 51.6 us -> 46.3 us (0.90)
  local copies, waits for them, and re-layouts: 4.36 us -> 0.86 us
  Pallas kernels: 45.7 us -> 42.2 us
  other arithmetic: 0 us -> 1.6 us
    unnamed x9 -> x6, local copies, waits for them, and re-layouts: 3.65 us -> 0.01 us
    pallas_call x1, Pallas kernels: 45.7 us -> 42.2 us  [per_device(): pl.pallas_call(functools.partial(kernel, nb, ng, dims, padded), out_shape...]
    add x0 -> x1, other arithmetic: none -> 1.6 us  [per_device(): new_residual + beta * direction]
    slice x0 -> x1, local copies, waits for them, and re-layouts: none -> 0.85 us  [per_device(): alpha, beta = (steps[0, :, 0:1], steps[1, :, 0:1])]
    broadcast_in_dim x1 -> x0, local copies, waits for them, and re-layouts: 0.71 us -> none  [per_device(): lengthscales[:, None]]
where the time goes in v2:
time: 46.3 us; the launch traced here: 46 us
  Pallas kernels  42.2 us (91%)
  other arithmetic  1.6 us (3%)
  between operations  1.33 us (3%)
  local copies, waits for them, and re-layouts  0.86 us (2%)
    pallas_call x1, Pallas kernels, per_device(): pl.pallas_call(functools.partial(kernel, nb, ng, dims, padded), out_shape...  42.2 us
    add x1, other arithmetic, per_device(): new_residual + beta * direction  1.6 us

profile of v2, /device:TPU:0, one launch (start us, length us, event | category | flops | bytes accessed | tf_op | source)
XLA Modules:
  0.0 46.0 jit_solution(17034490351874298767)
XLA Ops:
  1.3 0.0 copy-start
  1.3 0.0 copy-start.1
  1.3 0.0 copy-start.2
  1.3 42.2 %shard_map.85 = (f32[32,512]{1,0:T(8,128)}, f32[2,32,128]{2,1,0:T(8,128)}) custom-call(f32[54,512]{1,0:T(8,128)} %st_ref.1, f32[1,54]{1,0:T(1,128)} %bitcast.3, f32[1,1]{1,0:T(1,128)} %bitcast.2.nv_ref, f32[32,512]{1,0:T(8,128)} %res_ref.1, f32[32,512]{1,0:T(8,128)} %dir_ref.1), custom_call_target="tpu_custom_call" | custom-call | tf_op jit(solution)/shard_map/pallas_call | solution.py:335
  43.5 0.8 %slice_reduce_fusion = (f32[32]{0:T(128)S(1)}, f32[32]{0:T(128)S(1)}) fusion(f32[2,32,128]{2,1,0:T(8,128)} %get-tuple-element.5), kind=kLoop, calls=%fused_computation.3 | loop fusion | bytes 512 | tf_op jit(solution)/shard_map/slice | solution.py:362
  44.3 0.0 copy-done
  44.3 0.0 copy-done.1
  44.4 0.0 copy-done.2
  44.4 1.6 %multiply_add_fusion = (f32[32,512]{1,0:T(8,128)}, f32[32,512]{1,0:T(8,128)}, f32[32,512]{1,0:T(8,128)}) fusion(f32[32,512]{1,0:T(8,128)S(1)} %copy-done, f32[32]{0:T(128)S(1)} %get-tuple-element.7, f32[32,512]{1,0:T(8,128)S(1)} %copy-done.1, f32[32,512]{1,0:T(8,128)} %get-tuple-element.6, f32[32]{0:T(128)S(1)} %get-tuple-element.8, f32[32,512]{1,0:T(8,128)S(1)} %copy-done.2), kind=kLoop, calls=%fused_computation | loop fusion | flops 98304 | bytes 459008 | tf_op jit(solution)/shard_map/add | solution.py:364
Async XLA Ops:
  1.3 43.1 %copy-start = (f32[32,512]{1,0:T(8,128)S(1)}, f32[32,512]{1,0:T(8,128)}, u32[]{:S(2)}) copy-start(f32[32,512]{1,0:T(8,128)} %dir_ref.1) | copy-start | bytes 196612
  1.3 43.1 %copy-start.1 = (f32[32,512]{1,0:T(8,128)S(1)}, f32[32,512]{1,0:T(8,128)}, u32[]{:S(2)}) copy-start(f32[32,512]{1,0:T(8,128)} %res_ref.1) | copy-start | bytes 196612
  1.3 43.1 %copy-start.2 = (f32[32,512]{1,0:T(8,128)S(1)}, f32[32,512]{1,0:T(8,128)}, u32[]{:S(2)}) copy-start(f32[32,512]{1,0:T(8,128)} %param.9) | copy-start | bytes 196612

commit v3 on v2

--- a/solution.py
+++ b/solution.py
@@ -76,7 +76,7 @@
 
 def kernel(
     nb, ng, dims, padded, st_ref, ls_ref, nv_ref, res_ref, dir_ref,
-    image_ref, steps_ref,
+    image_ref, alpha_ref, beta_ref,
     colbuf, rowbuf, acol, brow, dd, acc, outbuf, redbuf, sums, xbuf,
     csend, crecv, fsend, frecv, rsend, rrecv, isend, irecv, ssend, srecv,
 ):
@@ -104,7 +104,6 @@
     colbuf[0, 0, 0:dims, :] = (st_ref[...] - 0.5) / lengths * TO_T
     colbuf[0, 0, padded:, :] = dir_ref[...]
     acc[...] = jnp.zeros_like(acc)
-    pl.semaphore_wait(barrier, len(others))
 
     def direct(p):
         to = sibling if p is None else partner(q, p, pairs) * 2 + core
@@ -139,12 +138,6 @@
             send_sem=isend.at[r], recv_sem=irecv.at[r],
             device_id=(b, partner(g, r, ng)), device_id_type=MESH,
         )
-
-    direct(None).start()
-    if ng > 1:
-        row_copy(1).start()
-    for p in range(1, min(pairs, 3)):
-        direct(p).start()
 
     def prepare_rows(r, src):
         high, low = split(src)
@@ -226,25 +219,29 @@
             outbuf[r] = acc[r, 0:probes, :] + acc[r, probes:, :]
             image_copy(r).start()
 
+    pl.semaphore_wait(barrier, len(others))
+    direct(None).start()
+    if ng > 1:
+        row_copy(1).start()
+    for p in range(1, min(pairs, 3)):
+        direct(p).start()
+
     prepare_columns(0, 0)
     prepare_rows(0, colbuf[0, 0, 0:padded, :])
     arrival(colbuf.at[0, 0], colbuf.at[0, 1], crecv.at[0])
     prepare_columns(0, 1)
-    xbuf[0] = distance(0, 0)
-    seen = {("p", 0), ("r", 0)}
-    for s in range(1, 3):
-        p, r = order[s]
-        if ("r", r) not in seen:
-            rows_arrive(r)
-            if r + 1 < ng:
-                row_copy(r + 1).start()
-        if ("p", p) not in seen:
-            for k in range(1, min(pairs, 3)):
-                pass_on(k)
-            if pairs > 3:
-                direct(3).start()
-            columns_arrive(p)
-        seen |= {("p", p), ("r", r)}
+    accumulate(0, 0, distance(0, 0))
+    rows_arrive(1)
+    if ng > 2:
+        row_copy(2).start()
+    accumulate(0, 1, distance(0, 1))
+    for k in range(1, min(pairs, 3)):
+        pass_on(k)
+    if pairs > 3:
+        direct(3).start()
+    columns_arrive(1)
+    xbuf[0] = distance(1, 0)
+    columns_arrive(2)
 
     def two_steps(i, carry):
         s = 2 * i
@@ -257,7 +254,7 @@
         accumulate(p1, r1, xbuf[1])
         send_off(r0, flags0)
         send_off(r1, flags1)
-        for first, total, copy in ((3, ng, row_copy), (4, pairs, direct)):
+        for first, total, copy in ((2, ng, row_copy), (3, pairs, direct)):
             if first < total:
 
                 @pl.when(i + first < total)
@@ -271,7 +268,7 @@
         lax.fori_loop(0, jnp.minimum(2, count - 3 - s), ready, 0)
         return carry
 
-    lax.fori_loop(0, count // 2 - 1, two_steps, 0)
+    lax.fori_loop(1, count // 2 - 1, two_steps, 0)
     (p0, r0), (p1, r1) = order[-2:]
     xbuf[1] = distance(p1, r1)
     accumulate(p0, r0, xbuf[0])
@@ -306,8 +303,10 @@
     rr, curv, ri, ii = [totals[k * probes : (k + 1) * probes, :] for k in range(4)]
     alpha = rr / curv
     fresh = rr - 2.0 * alpha * ri + alpha * alpha * ii
-    steps_ref[0] = alpha
-    steps_ref[1] = fresh / rr
+    beta = fresh / rr
+    for k in range(n // 128):
+        alpha_ref[:, k * 128 : (k + 1) * 128] = alpha
+        beta_ref[:, k * 128 : (k + 1) * 128] = beta
 
     direct(None).wait_send()
     for k in range(1, pairs):
@@ -332,14 +331,15 @@
         vmem = pl.BlockSpec(memory_space=pltpu.VMEM)
         smem = pl.BlockSpec(memory_space=pltpu.SMEM)
         dma = pltpu.SemaphoreType.DMA
-        image, steps = pl.pallas_call(
+        image, alpha, beta = pl.pallas_call(
             functools.partial(kernel, nb, ng, dims, padded),
             out_shape=(
                 jax.ShapeDtypeStruct((probes, n), F32),
-                jax.ShapeDtypeStruct((2, probes, 128), F32),
+                jax.ShapeDtypeStruct((probes, n), F32),
+                jax.ShapeDtypeStruct((probes, n), F32),
             ),
             in_specs=[vmem, vmem, smem, vmem, vmem],
-            out_specs=(vmem, vmem),
+            out_specs=(vmem, vmem, vmem),
             scratch_shapes=[
                 pltpu.VMEM((pairs, 2, padded + probes, n), F32),
                 pltpu.VMEM((ng, padded, n), F32),
@@ -359,7 +359,6 @@
                 collective_id=0, has_side_effects=True, vmem_limit_bytes=56 * 2**20
             ),
         )(states, lengthscales[None, :], noise_var[:, None], residual, direction)
-        alpha, beta = steps[0, :, 0:1], steps[1, :, 0:1]
         new_residual = residual - alpha * image
         return solution + alpha * direction, new_residual, new_residual + beta * direction
 

time: 46.3 us -> 44.9 us (0.970)
  local copies, waits for them, and re-layouts: 0.86 us -> 0.01 us
  Pallas kernels: 42.2 us -> 41.7 us
    slice x1 -> x0, local copies, waits for them, and re-layouts: 0.85 us -> none  [per_device(): alpha, beta = (steps[0, :, 0:1], steps[1, :, 0:1])]
    pallas_call x1, Pallas kernels: 42.2 us -> 41.7 us  [per_device(): pl.pallas_call(functools.partial(kernel, nb, ng, dims, padded), out_shape...]
where the time goes in v3:
time: 44.9 us; the launch traced here: 44.7 us
  Pallas kernels  41.7 us (93%)
  other arithmetic  1.6 us (4%)
  between operations  1.33 us (3%)
    pallas_call x1, Pallas kernels, per_device(): pl.pallas_call(functools.partial(kernel, nb, ng, dims, padded), out_shape...  41.7 us
    add x1, other arithmetic, per_device(): new_residual + beta * direction  1.6 us

profile of v3, /device:TPU:0, one launch (start us, length us, event | category | flops | bytes accessed | tf_op | source)
XLA Modules:
  0.0 44.7 jit_solution(5062512759243079420)
XLA Ops:
  1.3 0.0 copy-start
  1.3 0.0 copy-start.1
  1.3 0.0 copy-start.2
  1.3 41.7 %shard_map.85 = (f32[32,512]{1,0:T(8,128)}, f32[32,512]{1,0:T(8,128)}, f32[32,512]{1,0:T(8,128)}) custom-call(f32[54,512]{1,0:T(8,128)} %st_ref.1, f32[1,54]{1,0:T(1,128)} %bitcast.3, f32[1,1]{1,0:T(1,128)} %bitcast.2.nv_ref, f32[32,512]{1,0:T(8,128)} %res_ref.1, f32[32,512]{1,0:T(8,128)} %dir_ref.1), custom_call_target="tpu_custom_call" | custom-call | tf_op jit(solution)/shard_map/pallas_call | solution.py:334
  43.0 0.0 copy-done
  43.0 0.0 copy-done.1
  43.0 0.0 copy-done.2
  43.0 1.6 %multiply_add_fusion = (f32[32,512]{1,0:T(8,128)}, f32[32,512]{1,0:T(8,128)}, f32[32,512]{1,0:T(8,128)}) fusion(f32[32,512]{1,0:T(8,128)} %get-tuple-element.8, f32[32,512]{1,0:T(8,128)S(1)} %copy-done.1, f32[32,512]{1,0:T(8,128)S(1)} %copy-done, f32[32,512]{1,0:T(8,128)} %get-tuple-element.6, f32[32,512]{1,0:T(8,128)} %get-tuple-element.7, ...), kind=kLoop, calls=%fused_computation | loop fusion | flops 98304 | bytes 589824 | tf_op jit(solution)/shard_map/add | solution.py:363
Async XLA Ops:
  1.3 41.7 %copy-start = (f32[32,512]{1,0:T(8,128)S(1)}, f32[32,512]{1,0:T(8,128)}, u32[]{:S(2)}) copy-start(f32[32,512]{1,0:T(8,128)} %res_ref.1) | copy-start | bytes 196612
  1.3 41.7 %copy-start.1 = (f32[32,512]{1,0:T(8,128)S(1)}, f32[32,512]{1,0:T(8,128)}, u32[]{:S(2)}) copy-start(f32[32,512]{1,0:T(8,128)} %dir_ref.1) | copy-start | bytes 196612
  1.3 41.7 %copy-start.2 = (f32[32,512]{1,0:T(8,128)S(1)}, f32[32,512]{1,0:T(8,128)}, u32[]{:S(2)}) copy-start(f32[32,512]{1,0:T(8,128)} %param.9) | copy-start | bytes 196612
